TPU v7x, 32 devices: a whole 2x2x4 slice. The times are simulated.
32 devices in a mesh: gx: 4 (over x, core), gy: 2 (over y), gz: 4 (over z).
Axes of the slice: x: 2, y: 2, z: 4, core: 2. Of those that a mesh axis runs over, the one named last changes fastest.
Arguments:
- bead_pos: float32 [3, 8, 8, 8, 128], P(None, 'gx', 'gy', 'gz'), may hold values from 0 to 3
- bead_vel: float32 [3, 8, 8, 8, 128], P(None, 'gx', 'gy', 'gz'), may hold values from -6 to 6
- bead_force: float32 [3, 8, 8, 8, 128], P(None, 'gx', 'gy', 'gz'), may hold values from -60 to 60
- cell_count: int32 [8, 8, 8], P('gx', 'gy', 'gz'), may hold values from 0 to 128
- pair_seed: int32 [8, 8, 8, 128], P('gx', 'gy', 'gz'), may hold values from 0 to 4095
- bead_half: int32 [8, 8, 8, 128], P('gx', 'gy', 'gz'), may hold values from 0 to 1
- grid_vel: float32 [3, 8, 8, 16], P(None, 'gx', ('gy', 'gz')), may hold values from -6 to 6
- correlation_map: int32 [8, 8, 16], P('gx', ('gy', 'gz')), may hold values 0 or 1
Outputs:
- new_positions: float32 [3, 8, 8, 8, 128], P(None, 'gx', 'gy', 'gz')
- new_velocities: float32 [3, 8, 8, 8, 128], P(None, 'gx', 'gy', 'gz')
- grid_velocity: float32 [3, 8, 8, 16], P(None, 'gx', ('gy', 'gz'))
- pressure: float32 [8, 8, 16], P('gx', ('gy', 'gz'))
- brick_velocity: float32 [3, 8, 8, 16], P(None, 'gx', 'gy', 'gz')
Inputs may be any that keep to these rules, and one draw needn't show every extreme that they name: `cell_count`: slots below a cell's count hold beads, the others are padding.
All inputs are finite; a program needn't handle non-finite values. No bound on the sum of `correlation_map` on one device may be relied on, other than what follows from the above.
Results may differ from a plain program's by a relative error of at most 0.0003.
Values sent between devices are 32-bit elements; how exact they have to be, the bound alone decides.
A program may use at most 64 MiB of HBM per device.

v0:
```python
import functools
import math

import jax
import jax.numpy as jnp
from jax import lax
from jax.experimental import pallas as pl
from jax.experimental.pallas import tpu as pltpu
from jax.sharding import PartitionSpec as P

STEPS = 2
ITERS = 4

cell_edge = 3.0
conserve = 25.0
friction = 4.5
noise_scale = 3.0 * math.sqrt(12.0) / math.sqrt(0.04)
time_step = 0.04
predict_weight = 0.65
couple_rate = 0.5
hash_prime = 4093

LANES = 128
ROWS = 8
BLOCK = 32
FAR = 1.0e15
NEAR = [(ox, oy, oz) for ox in (-1, 0, 1) for oy in (-1, 0, 1) for oz in (-1, 0, 1)]


VMEM_SPEC = pl.BlockSpec(memory_space=pltpu.VMEM)
SMEM_SPEC = pl.BlockSpec(memory_space=pltpu.SMEM)


def pair_terms(own, chunk, step_tag):
    deltas = [own[k] - chunk[k] for k in range(3)]
    square = deltas[0] * deltas[0] + deltas[1] * deltas[1] + deltas[2] * deltas[2]
    weight = jnp.maximum(1.0 - square, 0.0)
    closing = deltas[0] * (own[3] - chunk[3])
    closing = closing + deltas[1] * (own[4] - chunk[4])
    closing = closing + deltas[2] * (own[5] - chunk[5])
    turns = own[6] * chunk[6] + (0.5 - step_tag * step_tag) / hash_prime
    part = turns - jnp.floor(turns)
    steady = part * noise_scale + (conserve - (0.5 + 0.5 / hash_prime) * noise_scale)
    strength = weight * (steady - weight * closing)
    return [strength * deltas[k] for k in range(3)]


def centred(seed, step_tag):
    moved = seed + float(step_tag)
    return jnp.where(moved > 2046.0, moved - float(hash_prime), moved)


def select_beads(padded_ref, rows_x, masks, index_ref, base_ref):
    px, py, pz = padded_ref.shape[:3]
    cx, cy, cz = px - 2, py - 2, pz - 2
    cells = cx * cy * cz
    for ix in range(px):
        for iz in range(pz):
            present = padded_ref[ix, :, iz, 7, :] > 0.5
            for k in range(3):
                rows_x[k, ix, iz, 0:py, :] = jnp.where(present, padded_ref[ix, :, iz, k, :], FAR)

    for ix in range(cx):
        for iz in range(cz):
            row = (ix * cz + iz) * cy
            low, high = [], []
            for k in range(3):
                mine = rows_x[k, 1 + ix, 1 + iz, 1 : 1 + cy, :]
                there = mine < 0.1 * FAR
                least = jnp.min(jnp.where(there, mine, FAR), axis=1, keepdims=True)
                most = jnp.max(jnp.where(there, mine, -FAR), axis=1, keepdims=True)
                low.append(least - 1.001 - 1e-6 * jnp.abs(least))
                high.append(most + 1.001 + 1e-6 * jnp.abs(most))
            for n, offset in enumerate(NEAR):
                keep = None
                for k in range(3):
                    near = rows_x[
                        k, 1 + ix + offset[0], 1 + iz + offset[2], 1 + offset[1] : 1 + offset[1] + cy, :
                    ]
                    shift = cell_edge * offset[k]
                    inside = (near >= low[k] - shift) & (near <= high[k] - shift)
                    keep = inside if keep is None else keep & inside
                masks[n * cells + row : n * cells + row + cy, :] = jnp.where(keep, 1.0, 0.0)

    mask = masks[...]
    before = lax.broadcasted_iota(jnp.int32, (LANES, LANES), 0)
    after = lax.broadcasted_iota(jnp.int32, (LANES, LANES), 1)
    upper = jnp.where(before < after, 1.0, 0.0).astype(jnp.bfloat16)
    ones = jnp.ones((LANES, LANES), jnp.bfloat16)
    mask16 = mask.astype(jnp.bfloat16)
    rank = jnp.dot(mask16, upper, preferred_element_type=jnp.float32).astype(jnp.int32)
    count = jnp.dot(mask16, ones, preferred_element_type=jnp.float32).astype(jnp.int32)
    spot = lax.broadcasted_iota(jnp.int32, mask.shape, 1)
    entry = jnp.where(mask > 0.5, (spot - rank) * LANES + spot, spot)
    for bit in range(7):
        width = 1 << bit
        flag = LANES << bit
        moved = pltpu.roll(entry, LANES - width, 1)
        stay = jnp.where((entry & flag) != 0, entry & (LANES - 1), entry)
        entry = jnp.where((moved & flag) != 0, moved, stay)
    entry = entry & (LANES - 1)
    bases = []
    running = jnp.zeros((cells, LANES), jnp.int32)
    table = jnp.zeros((cells, LANES), jnp.int32)
    spot_cells = lax.broadcasted_iota(jnp.int32, (cells, LANES), 1)
    for n in range(len(NEAR)):
        bases.append(running)
        table = jnp.where(spot_cells == n, running, table)
        running = running + count[n * cells : (n + 1) * cells, :]
    base_ref[...] = jnp.where(spot_cells == len(NEAR), running, table)
    base_all = jnp.concatenate(bases, axis=0)
    for bit in range(7):
        width = 1 << bit
        entry = jnp.where((base_all & width) != 0, pltpu.roll(entry, width, 1), entry)
    index_ref[...] = entry


def force_kernel(step_tag, phase, count_ref, padded_ref, state_ref, *refs):
    if phase == 0:
        tile_out, index_ref, base_ref, *scratch = refs
    elif phase == 1:
        index_ref, base_ref, tile_out, state_out, *scratch = refs
    else:
        index_ref, base_ref, state_out, pos_out, vel_out, *scratch = refs
    rows_x, masks, shifts, base_smem, list_ref, own_wide, force_wide, copy_sem = scratch
    px, py, pz = padded_ref.shape[:3]
    cx, cy, cz = px - 2, py - 2, pz - 2
    cells = cx * cy * cz
    if phase == 0:
        select_beads(padded_ref, rows_x, masks, index_ref, base_ref)
    to_smem = pltpu.make_async_copy(base_ref, base_smem, copy_sem)
    to_smem.start()
    lane = lax.broadcasted_iota(jnp.int32, (ROWS, LANES), 1)
    row_id = lax.broadcasted_iota(jnp.int32, (ROWS, LANES), 0)
    for n, offset in enumerate(NEAR):
        shift = jnp.zeros((ROWS, LANES), jnp.float32)
        for k in range(3):
            shift = jnp.where(row_id == k, cell_edge * offset[k], shift)
        shifts[n] = shift
    eye = lax.broadcasted_iota(jnp.int32, (LANES, LANES), 0) == lax.broadcasted_iota(
        jnp.int32, (LANES, LANES), 1
    )
    zero = jnp.zeros((BLOCK, LANES), jnp.float32)
    to_smem.wait()

    def one_cell(cell, carry):
        ix = cell // (cy * cz)
        iz = (cell // cy) % cz
        iy = cell % cy
        current = jnp.zeros((ROWS, LANES), jnp.float32)
        for n, offset in enumerate(NEAR):
            tile = padded_ref[ix + 1 + offset[0], iy + 1 + offset[1], iz + 1 + offset[2]]
            index = jnp.broadcast_to(index_ref[pl.ds(n * cells + cell, 1), :], (ROWS, LANES))
            found = jnp.take_along_axis(tile, index, axis=1) + shifts[n]
            base = base_smem[cell, n]
            following = base_smem[cell, n + 1]
            merged = jnp.where(lane >= (base & (LANES - 1)), found, current)
            list_ref[base >> 7] = merged
            crossed = (following >> 7) > (base >> 7)
            current = jnp.where(crossed, found, merged)
        total = base_smem[cell, len(NEAR)]
        list_ref[total >> 7] = jnp.where(
            (row_id == 0) & (lane >= (total & (LANES - 1))), -FAR, current
        )
        chunks = (total + LANES - 1) >> 7
        own_tile = padded_ref[ix + 1, iy + 1, iz + 1]
        own_cols = own_tile.T
        for k in range(7):
            own_wide[k] = jnp.broadcast_to(own_cols[:, k : k + 1], (LANES, LANES))
        blocks = (count_ref[ix, iy, iz] + BLOCK - 1) // BLOCK

        def one_block(block, carry):
            at = pl.multiple_of(block * BLOCK, BLOCK)
            own = [own_wide[k, pl.ds(at, BLOCK), :] for k in range(7)]
            own[6] = own[6] * (1.0 / hash_prime)

            def one_chunk(index, sums):
                chunk = [list_ref[index, k : k + 1, :] for k in range(7)]
                terms = pair_terms(own, chunk, step_tag)
                return tuple(sums[k] + terms[k] for k in range(3))

            sums = lax.fori_loop(0, chunks, one_chunk, (zero, zero, zero))
            for k in range(3):
                force_wide[k, pl.ds(at, BLOCK), :] = sums[k]
            return carry

        lax.fori_loop(0, blocks, one_block, 0)
        state = state_ref[ix, iy, iz]
        new_vel, force = [], []
        for k in range(3):
            column = jnp.sum(force_wide[k], axis=1, keepdims=True)
            row = jnp.sum(jnp.where(eye, column, 0.0), axis=0, keepdims=True)
            row = jnp.where(own_tile[7:8, :] > 0.5, row, 0.0)
            force.append(row)
            new_vel.append(
                state[k : k + 1, :] + 0.5 * time_step * (state[3 + k : 4 + k, :] + row)
            )
        if phase == 0:
            for k in range(3):
                tile_out[ix, iy, iz, k : k + 1, :] = own_tile[k : k + 1, :]
                tile_out[ix, iy, iz, 3 + k : 4 + k, :] = friction * new_vel[k]
            tile_out[ix, iy, iz, 6:8, :] = own_tile[6:8, :]
            return carry
        for k in range(3):
            state_out[ix, iy, iz, k : k + 1, :] = new_vel[k]
            state_out[ix, iy, iz, 3 + k : 4 + k, :] = force[k]
        state_out[ix, iy, iz, 6:8, :] = state[6:8, :]
        for k in range(3):
            position = own_tile[k : k + 1, :]
            if phase == 2:
                pos_out[k, ix, iy, pl.ds(iz, 1), :] = position
                vel_out[k, ix, iy, pl.ds(iz, 1), :] = new_vel[k]
                continue
            position = position + time_step * new_vel[k]
            position = position + 0.5 * time_step * time_step * force[k]
            tile_out[ix, iy, iz, k : k + 1, :] = position
            guessed = new_vel[k] + predict_weight * time_step * force[k]
            tile_out[ix, iy, iz, 3 + k : 4 + k, :] = friction * guessed
        if phase == 1:
            tile_out[ix, iy, iz, 6:7, :] = centred(state[6:7, :], step_tag + 1)
            tile_out[ix, iy, iz, 7:8, :] = state[7:8, :]
        return carry

    lax.fori_loop(0, cells, one_cell, 0)


def force_call(step_tag, phase, cell_count, padded, state, *selection):
    px, py, pz = padded.shape[:3]
    cx, cy, cz = state.shape[:3]
    cells = cx * cy * cz
    near = len(NEAR)
    tall = -(-py // 8) * 8
    brick = jax.ShapeDtypeStruct(state.shape, jnp.float32)
    beads = jax.ShapeDtypeStruct((3, cx, cy, cz, LANES), jnp.float32)
    if phase == 0:
        index = jax.ShapeDtypeStruct((near * cells, LANES), jnp.int32)
        outs = (brick, index, jax.ShapeDtypeStruct((cells, LANES), jnp.int32))
    else:
        outs = (brick, brick) if phase == 1 else (brick, beads, beads)
    return pl.pallas_call(
        functools.partial(force_kernel, step_tag, phase),
        out_shape=outs,
        in_specs=[SMEM_SPEC] + [VMEM_SPEC] * (2 + len(selection)),
        out_specs=(VMEM_SPEC,) * len(outs),
        scratch_shapes=[
            pltpu.VMEM((3, px, pz, tall, LANES), jnp.float32),
            pltpu.VMEM((near * cells, LANES), jnp.float32),
            pltpu.VMEM((near, ROWS, LANES), jnp.float32),
            pltpu.SMEM((cells, LANES), jnp.int32),
            pltpu.VMEM((near + 1, ROWS, LANES), jnp.float32),
            pltpu.VMEM((7, LANES, LANES), jnp.float32),
            pltpu.VMEM((3, LANES, LANES), jnp.float32),
            pltpu.SemaphoreType.DMA,
        ],
        compiler_params=pltpu.CompilerParams(vmem_limit_bytes=32 * 1024 * 1024),
        name="pair_forces",
    )(cell_count, padded, state, *selection)


MESH = pl.DeviceIdType.MESH
AROUND = [offset for offset in NEAR if offset != (0, 0, 0)]


def when(condition, body):
    if condition is None:
        body()
    else:
        pl.when(condition)(body)


def beside(offset, sizes):
    nx, ny, nz = sizes
    target = (
        lax.rem(lax.axis_index("gx") + (offset[0] + nx), nx),
        lax.axis_index("gy") + offset[1],
        lax.axis_index("gz") + offset[2],
    )
    exists = None
    for step, place, size in ((offset[1], target[1], ny), (offset[2], target[2], nz)):
        if step != 0:
            inside = place >= 0 if step < 0 else place < size
            exists = inside if exists is None else exists & inside
    return target, exists


def source_slice(step, count):
    return pl.ds(0, count) if step == 0 else pl.ds(count - 1 if step > 0 else 0, 1)


def halo_slice(step, count):
    return pl.ds(1, count) if step == 0 else pl.ds(0 if step > 0 else count + 1, 1)


def exchange_body(sizes, fill, source_ref, padded_ref, send_sems, recv_sems):
    extent = tuple(size - 2 for size in padded_ref.shape[:3])
    barrier = pltpu.get_barrier_semaphore()
    places = {offset: beside(offset, sizes) for offset in AROUND}
    for offset in AROUND:
        target, exists = places[offset]

        def greet(target=target):
            pl.semaphore_signal(barrier, inc=1, device_id=target, device_id_type=MESH)

        when(exists, greet)
    fill()
    copies = {}
    for number, offset in enumerate(AROUND):
        target, exists = places[offset]
        back = tuple(-step for step in offset)
        area = tuple(halo_slice(back[k], extent[k]) for k in range(3))
        if exists is not None:

            def blank(area=area):
                shape = tuple(part.size for part in area) + padded_ref.shape[3:]
                padded_ref[area] = jnp.zeros(shape, jnp.float32)

            pl.when(jnp.logical_not(exists))(blank)
        copies[offset] = pltpu.make_async_remote_copy(
            src_ref=source_ref.at[tuple(source_slice(offset[k], extent[k]) for k in range(3))],
            dst_ref=padded_ref.at[tuple(halo_slice(offset[k], extent[k]) for k in range(3))],
            send_sem=send_sems.at[number],
            recv_sem=recv_sems.at[number],
            device_id=target,
            device_id_type=MESH,
        )
    around = 3
    for axis, size in (("gy", sizes[1]), ("gz", sizes[2])):
        place = lax.axis_index(axis)
        around = around * (1 + jnp.minimum(place, 1) + jnp.minimum(size - 1 - place, 1))
    pl.semaphore_wait(barrier, around - 1)
    for offset in AROUND:
        when(places[offset][1], copies[offset].start)
    for offset in AROUND:
        back = tuple(-step for step in offset)
        when(places[back][1], copies[offset].wait_recv)
    for offset in AROUND:
        when(places[offset][1], copies[offset].wait_send)


def exchange_kernel(sizes, tile_ref, padded_ref, send_sems, recv_sems):
    cx, cy, cz = tile_ref.shape[:3]

    def fill():
        padded_ref[1 : 1 + cx, 1 : 1 + cy, 1 : 1 + cz] = tile_ref[...]

    exchange_body(sizes, fill, tile_ref, padded_ref, send_sems, recv_sems)


def first_kernel(
    sizes, count_ref, pos_ref, vel_ref, force_ref, seed_ref, padded_ref, state_ref,
    tile_ref, send_sems, recv_sems,
):
    cx, cy, cz = tile_ref.shape[:3]
    slot = lax.broadcasted_iota(jnp.int32, (1, LANES), 1)

    def fill():
        for ix in range(cx):
            for iy in range(cy):
                for iz in range(cz):
                    pos, vel, force = [
                        ref[:, ix, iy, iz, :] for ref in (pos_ref, vel_ref, force_ref)
                    ]
                    seed = seed_ref[ix, iy, iz : iz + 1, :].astype(jnp.float32)
                    here = jnp.where(slot < count_ref[ix, iy, iz], 1.0, 0.0)
                    pos = pos + time_step * vel + 0.5 * time_step * time_step * force
                    guessed = vel + predict_weight * time_step * force
                    for ref, top, low, mark in (
                        (tile_ref, pos, friction * guessed, centred(seed, 3)),
                        (state_ref, vel, force, seed),
                    ):
                        ref[ix, iy, iz, 0:3, :] = top
                        ref[ix, iy, iz, 3:6, :] = low
                        ref[ix, iy, iz, 6:7, :] = mark
                        ref[ix, iy, iz, 7:8, :] = here
        padded_ref[1 : 1 + cx, 1 : 1 + cy, 1 : 1 + cz] = tile_ref[...]

    exchange_body(sizes, fill, tile_ref, padded_ref, send_sems, recv_sems)


def mesh_sizes():
    return tuple(lax.axis_size(axis) for axis in ("gx", "gy", "gz"))


def padded_shape(extent):
    return tuple(size + 2 for size in extent) + (ROWS, LANES)


def exchange_sems():
    return [pltpu.SemaphoreType.DMA((len(AROUND),)), pltpu.SemaphoreType.DMA((len(AROUND),))]


def comm_params(number):
    return pltpu.CompilerParams(
        collective_id=number, has_side_effects=True, vmem_limit_bytes=32 * 1024 * 1024
    )


def exchange_call(tile):
    return pl.pallas_call(
        functools.partial(exchange_kernel, mesh_sizes()),
        out_shape=jax.ShapeDtypeStruct(padded_shape(tile.shape[:3]), jnp.float32),
        in_specs=[VMEM_SPEC],
        out_specs=VMEM_SPEC,
        scratch_shapes=exchange_sems(),
        compiler_params=comm_params(1),
        name="exchange",
    )(tile)


def first_call(cell_count, bead_pos, bead_vel, bead_force, pair_seed):
    extent = cell_count.shape
    return pl.pallas_call(
        functools.partial(first_kernel, mesh_sizes()),
        out_shape=(
            jax.ShapeDtypeStruct(padded_shape(extent), jnp.float32),
            jax.ShapeDtypeStruct(extent + (ROWS, LANES), jnp.float32),
        ),
        in_specs=[SMEM_SPEC] + [VMEM_SPEC] * 4,
        out_specs=(VMEM_SPEC, VMEM_SPEC),
        scratch_shapes=[pltpu.VMEM(extent + (ROWS, LANES), jnp.float32)] + exchange_sems(),
        compiler_params=comm_params(2),
        name="first_exchange",
    )(cell_count, bead_pos, bead_vel, bead_force, pair_seed)


def gather_kernel(
    sizes, state_ref, half_ref, grid_ref, map_ref, whole,
    mine, along_z, along_y, slots_z, slots_y, send_sems, recv_sems,
):
    nx, ny, nz = sizes
    cx, cy, cz = state_ref.shape[:3]
    rows, depth = grid_ref.shape[2:]
    span = mine.shape[2]
    count_y = span // depth
    here = (lax.axis_index("gx"), lax.axis_index("gy"), lax.axis_index("gz"))
    barrier = pltpu.get_barrier_semaphore()
    peers = []
    for axis, size in ((2, nz), (1, ny), (0, nx)):
        for step in range(1, size):
            target = list(here)
            target[axis] = lax.rem(here[axis] + step, size)
            peers.append((axis, step, tuple(target)))
    for axis, step, target in peers:
        pl.semaphore_signal(barrier, inc=1, device_id=target, device_id_type=MESH)

    lane = lax.broadcasted_iota(jnp.int32, (ROWS, span), 1)
    row_id = lax.broadcasted_iota(jnp.int32, (ROWS, LANES), 0)
    for ix in range(cx):
        placed = jnp.zeros((ROWS, span), jnp.float32)
        for row in range(rows):
            mine[ix] = jnp.zeros((ROWS, span), jnp.float32)
            for k in range(3):
                mine[ix, 4 + k : 5 + k, 0:depth] = grid_ref[k, ix, row : row + 1, :]
            mine[ix, 7:8, 0:depth] = map_ref[ix, row : row + 1, :].astype(jnp.float32)
            at = ((here[1] * nz + here[2]) * rows + row) * depth
            placed = placed + pltpu.roll(mine[ix], at, 1)
        for iy in range(cy):
            for iz in range(cz):
                tile = state_ref[ix, iy, iz]
                values = jnp.where(row_id < 3, tile, jnp.where(row_id == 3, 1.0, 0.0))
                values = jnp.where(tile[7:8, :] > 0.5, values, 0.0)
                half = half_ref[ix, iy, iz : iz + 1, :]
                for side in (0, 1):
                    total = jnp.sum(
                        jnp.where(half == side, values, 0.0), axis=1, keepdims=True
                    )
                    at = (here[1] * cy + iy) * depth + (here[2] * cz + iz) * 2 + side
                    placed = placed + jnp.where(lane == at, total, 0.0)
        mine[ix] = placed

    pl.semaphore_wait(barrier, len(peers))
    number = 0
    for axis, source, slots, size, result in (
        (2, mine, slots_z, nz, along_z),
        (1, along_z, slots_y, ny, along_y),
        (0, along_y, None, nx, None),
    ):
        copies = []
        for peer_axis, step, target in peers:
            if peer_axis != axis:
                continue
            if axis == 0:
                landing = whole.at[pl.ds(here[0] * cx, cx)]
            else:
                landing = slots.at[step - 1]
            copies.append(
                pltpu.make_async_remote_copy(
                    src_ref=source,
                    dst_ref=landing,
                    send_sem=send_sems.at[number],
                    recv_sem=recv_sems.at[number],
                    device_id=target,
                    device_id_type=MESH,
                )
            )
            number += 1
        for copy in copies:
            copy.start()
        if axis == 0:
            whole[pl.ds(here[0] * cx, cx)] = source[...]
        for copy in copies:
            copy.wait()
        if axis != 0:
            total = source[...]
            for step in range(1, size):
                total = total + slots[step - 1]
            result[...] = total


def project_kernel(sizes, extent, rows, depth, whole, grid_out, pressure_out, brick_out, fields):
    nx, ny, nz = sizes
    cx, cy, cz = extent
    span = whole.shape[2]
    count_y = span // depth
    here = (lax.axis_index("gx"), lax.axis_index("gy"), lax.axis_index("gz"))
    parts = [whole[:, k, :] for k in range(8)]
    lanes = lax.broadcasted_iota(jnp.int32, parts[0].shape, 1)
    place_z = lax.rem(lanes, depth)
    place_y = lanes // depth
    count_x = parts[0].shape[0]

    def after(field, axis):
        if axis == 0:
            return pltpu.roll(field, count_x - 1, 0)
        if axis == 1:
            return jnp.where(place_y == count_y - 1, 0.0, pltpu.roll(field, span - depth, 1))
        return jnp.where(place_z == depth - 1, 0.0, pltpu.roll(field, span - 1, 1))

    def prior(field, axis):
        if axis == 0:
            return pltpu.roll(field, 1, 0)
        if axis == 1:
            return jnp.where(place_y == 0, 0.0, pltpu.roll(field, depth, 1))
        return jnp.where(place_z == 0, 0.0, pltpu.roll(field, 1, 1))

    def total_of(field):
        return jnp.sum(jnp.sum(field, axis=0, keepdims=True), axis=1, keepdims=True)

    share = jnp.maximum(parts[3], 1.0)
    coupled = [
        parts[4 + k] + couple_rate * parts[7] * (parts[k] / share - parts[4 + k])
        for k in range(3)
    ]
    divergence = 0.0
    for k in range(3):
        divergence = divergence + after(coupled[k], k) - prior(coupled[k], k)
    residual = -0.5 * divergence
    direction = residual
    pressure = jnp.zeros_like(residual)
    norm_now = total_of(residual * residual)
    for repeat in range(ITERS):
        around = 0.0
        for k in range(3):
            around = around + after(direction, k) + prior(direction, k)
        applied = 6.0 * direction - around
        step_length = norm_now / total_of(direction * applied)
        pressure = pressure + step_length * direction
        residual = residual - step_length * applied
        norm_next = total_of(residual * residual)
        direction = residual + norm_next / norm_now * direction
        norm_now = norm_next
    for k in range(3):
        fields[:, k, :] = coupled[k] - 0.5 * (after(pressure, k) - prior(pressure, k))
    fields[:, 3, :] = pressure
    for ix in range(cx):
        own = fields[here[0] * cx + ix]
        for row in range(rows):
            start = ((here[1] * nz + here[2]) * rows + row) * depth
            band = pltpu.roll(own, lax.rem(span - start, span), 1)
            for k in range(3):
                grid_out[k, ix, row : row + 1, :] = band[k : k + 1, 0:depth]
            pressure_out[ix, row : row + 1, :] = band[3:4, 0:depth]
        for iy in range(cy):
            start = (here[1] * cy + iy) * depth + here[2] * cz * 2
            band = pltpu.roll(own, lax.rem(span - start, span), 1)
            for k in range(3):
                brick_out[k, ix, iy : iy + 1, :] = band[k : k + 1, 0 : cz * 2]


def project_call(state, bead_half, grid_vel, correlation_map):
    sizes = mesh_sizes()
    nx, ny, nz = sizes
    cx, cy, cz = state.shape[:3]
    depth = grid_vel.shape[3]
    span = ny * cy * depth
    shape = (cx, ROWS, span)
    peers = nx + ny + nz - 3
    whole = jax.ShapeDtypeStruct((nx * cx, ROWS, span), jnp.float32)
    gathered = pl.pallas_call(
        functools.partial(gather_kernel, sizes),
        out_shape=whole,
        in_specs=[VMEM_SPEC] * 4,
        out_specs=VMEM_SPEC,
        scratch_shapes=[
            pltpu.VMEM(shape, jnp.float32),
            pltpu.VMEM(shape, jnp.float32),
            pltpu.VMEM(shape, jnp.float32),
            pltpu.VMEM((max(nz - 1, 1),) + shape, jnp.float32),
            pltpu.VMEM((max(ny - 1, 1),) + shape, jnp.float32),
            pltpu.SemaphoreType.DMA((max(peers, 1),)),
            pltpu.SemaphoreType.DMA((max(peers, 1),)),
        ],
        compiler_params=comm_params(3),
        name="gather_grid",
    )(state, bead_half, grid_vel, correlation_map)
    return pl.pallas_call(
        functools.partial(project_kernel, sizes, (cx, cy, cz), grid_vel.shape[2], depth),
        out_shape=(
            jax.ShapeDtypeStruct(grid_vel.shape, jnp.float32),
            jax.ShapeDtypeStruct(correlation_map.shape, jnp.float32),
            jax.ShapeDtypeStruct((3, cx, cy, cz * 2), jnp.float32),
        ),
        in_specs=[VMEM_SPEC],
        out_specs=(VMEM_SPEC,) * 3,
        scratch_shapes=[pltpu.VMEM(whole.shape, jnp.float32)],
        compiler_params=pltpu.CompilerParams(vmem_limit_bytes=32 * 1024 * 1024),
        name="project",
    )(gathered)


def per_device(
    bead_pos, bead_vel, bead_force, cell_count, pair_seed, bead_half, grid_vel, correlation_map
):
    padded, state = first_call(cell_count, bead_pos, bead_vel, bead_force, pair_seed)
    for step_number in range(STEPS):
        step_tag = step_number + 3
        if step_number > 0:
            padded = exchange_call(tile)
        tile, *selection = force_call(step_tag, 0, cell_count, padded, state)
        padded = exchange_call(tile)
        if step_number < STEPS - 1:
            tile, state = force_call(step_tag, 1, cell_count, padded, state, *selection)
    state, position, velocity = force_call(step_tag, 2, cell_count, padded, state, *selection)
    return (position, velocity, *project_call(state, bead_half, grid_vel, correlation_map))


def solution(mesh):
    placed = (
        P(None, "gx", "gy", "gz", None),
        P(None, "gx", "gy", "gz", None),
        P(None, "gx", "gy", "gz", None),
        P("gx", "gy", "gz"),
        P("gx", "gy", "gz", None),
        P("gx", "gy", "gz", None),
        P(None, "gx", ("gy", "gz"), None),
        P("gx", ("gy", "gz"), None),
    )
    return jax.shard_map(
        per_device,
        mesh=mesh,
        in_specs=placed,
        out_specs=(
            P(None, "gx", "gy", "gz", None),
            P(None, "gx", "gy", "gz", None),
            P(None, "gx", ("gy", "gz"), None),
            P("gx", ("gy", "gz"), None),
            P(None, "gx", "gy", "gz"),
        ),
        check_vma=False,
    )
```

profile of v0, /device:TPU:0, one launch (start us, length us, event | category | flops | bytes accessed | tf_op | source)
XLA Modules:
  0.0 103.2 jit_solution(10574211630165155051)
XLA Ops:
  0.6 0.8 copy.17.count_ref
  1.4 0.0 copy-start
  1.4 0.7 copy-done
  2.1 0.0 copy-start.1
  2.1 0.7 copy-done.1
  2.9 0.0 copy-start.2
  2.9 0.7 copy-done.2
  3.6 0.0 copy-start.4
  3.6 0.7 copy-done.4
  4.3 9.9 %first_exchange.1 = (f32[4,6,4,8,128]{4,3,2,1,0:T(8,128)S(1)}, f32[2,4,2,8,128]{4,3,2,1,0:T(8,128)S(1)}) custom-call(s32[2,4,2]{2,1,0:T(4,128)S(1)} %copy.17.count_ref, f32[3,2,4,2,128]{4,3,2,1,0:T(2,128)S(1)} %copy-done, f32[3,2,4,2,128]{4,3,2,1,0:T(2,128)S(1)} %copy-done.1, f32[3,2,4,2,128]{4,3,2,1,0:T(2,128)S(1)} %copy-done.2, s32[2,4,2,128]{3,2,1,0:T(2,128)S(1)} %copy-done.4), custom_call_target="tpu_custom_call" | custom-call | tf_op jit(solution)/shard_map/first_exchange/pallas_call | solution.py:412
  14.2 14.2 %pair_forces.4 = (f32[2,4,2,8,128]{4,3,2,1,0:T(8,128)S(1)}, s32[432,128]{1,0:T(8,128)S(1)}, s32[16,128]{1,0:T(8,128)S(1)}) custom-call(s32[2,4,2]{2,1,0:T(4,128)S(1)} %copy.17.count_ref, f32[4,6,4,8,128]{4,3,2,1,0:T(8,128)S(1)} %get-tuple-element.21.padded_ref, f32[2,4,2,8,128]{4,3,2,1,0:T(8,128)S(1)} %get-tuple-element.22.state_ref), custom_call_target="tpu_custom_call" | custom-call | tf_op jit(solution)/shard_map/pair_forces/pallas_call | solution.py:240
  28.4 6.9 %exchange.3.padded_ref = f32[4,6,4,8,128]{4,3,2,1,0:T(8,128)S(1)} custom-call(f32[2,4,2,8,128]{4,3,2,1,0:T(8,128)S(1)} %get-tuple-element.23.tile_ref), custom_call_target="tpu_custom_call" | custom-call | tf_op jit(solution)/shard_map/exchange/pallas_call | solution.py:399
  35.4 12.6 %pair_forces.5 = (f32[2,4,2,8,128]{4,3,2,1,0:T(8,128)S(1)}, f32[2,4,2,8,128]{4,3,2,1,0:T(8,128)S(1)}) custom-call(s32[2,4,2]{2,1,0:T(4,128)S(1)} %copy.17.count_ref, f32[4,6,4,8,128]{4,3,2,1,0:T(8,128)S(1)} %exchange.3.padded_ref, f32[2,4,2,8,128]{4,3,2,1,0:T(8,128)S(1)} %get-tuple-element.22.state_ref, s32[432,128]{1,0:T(8,128)S(1)} %get-tuple-element.24.refs_0_, ...), custom_call_target="tpu_custom_call" | custom-call | tf_op jit(solution)/shard_map/pair_forces/pallas_call | solution.py:240
  48.0 6.8 %exchange.4.padded_ref = f32[4,6,4,8,128]{4,3,2,1,0:T(8,128)S(1)} custom-call(f32[2,4,2,8,128]{4,3,2,1,0:T(8,128)S(1)} %get-tuple-element.26.tile_ref), custom_call_target="tpu_custom_call" | custom-call | tf_op jit(solution)/shard_map/exchange/pallas_call | solution.py:399
  54.8 14.3 %pair_forces.6 = (f32[2,4,2,8,128]{4,3,2,1,0:T(8,128)S(1)}, s32[432,128]{1,0:T(8,128)S(1)}, s32[16,128]{1,0:T(8,128)S(1)}) custom-call(s32[2,4,2]{2,1,0:T(4,128)S(1)} %copy.17.count_ref, f32[4,6,4,8,128]{4,3,2,1,0:T(8,128)S(1)} %exchange.4.padded_ref, f32[2,4,2,8,128]{4,3,2,1,0:T(8,128)S(1)} %get-tuple-element.27.state_ref), custom_call_target="tpu_custom_call" | custom-call | tf_op jit(solution)/shard_map/pair_forces/pallas_call | solution.py:240
  69.1 6.6 %exchange.5.padded_ref = f32[4,6,4,8,128]{4,3,2,1,0:T(8,128)S(1)} custom-call(f32[2,4,2,8,128]{4,3,2,1,0:T(8,128)S(1)} %get-tuple-element.28.tile_ref), custom_call_target="tpu_custom_call" | custom-call | tf_op jit(solution)/shard_map/exchange/pallas_call | solution.py:399
  75.7 0.0 copy-start.3
  75.8 13.3 %pair_forces.7 = (f32[2,4,2,8,128]{4,3,2,1,0:T(8,128)S(1)}, f32[3,2,4,2,128]{4,3,2,1,0:T(2,128)}, f32[3,2,4,2,128]{4,3,2,1,0:T(2,128)}) custom-call(s32[2,4,2]{2,1,0:T(4,128)S(1)} %copy.17.count_ref, f32[4,6,4,8,128]{4,3,2,1,0:T(8,128)S(1)} %exchange.5.padded_ref, f32[2,4,2,8,128]{4,3,2,1,0:T(8,128)S(1)} %get-tuple-element.27.state_ref, ...), custom_call_target="tpu_custom_call" | custom-call | tf_op jit(solution)/shard_map/pair_forces/pallas_call | solution.py:240
  89.0 0.0 copy-start.5
  89.0 0.0 copy-start.6
  89.0 0.0 copy-done.3
  89.1 0.7 copy-done.5
  89.7 0.0 copy-done.6
  89.7 11.7 %gather_grid.1.whole = f32[8,8,128]{2,1,0:T(8,128)S(1)} custom-call(f32[2,4,2,8,128]{4,3,2,1,0:T(8,128)S(1)} %get-tuple-element.33.state_ref, s32[2,4,2,128]{3,2,1,0:T(2,128)S(1)} %copy-done.3, f32[3,2,1,16]{3,2,1,0:T(1,128)S(1)} %copy-done.5, s32[2,1,16]{2,1,0:T(1,128)S(1)} %copy-done.6), custom_call_target="tpu_custom_call" | custom-call | tf_op jit(solution)/shard_map/gather_grid/pallas_call | solution.py:589
  101.4 1.8 %project.1 = (f32[3,2,1,16]{3,2,1,0:T(1,128)}, f32[2,1,16]{2,1,0:T(1,128)}, f32[3,2,4,4]{3,2,1,0:T(4,128)}) custom-call(f32[8,8,128]{2,1,0:T(8,128)S(1)} %gather_grid.1.whole), custom_call_target="tpu_custom_call" | custom-call | tf_op jit(solution)/shard_map/project/pallas_call | solution.py:606
Async XLA Ops:
  1.4 0.7 copy-start
  2.1 0.7 copy-start.1
  2.9 0.7 copy-start.2
  3.6 0.7 copy-start.4
  75.7 13.3 %copy-start.3 = (s32[2,4,2,128]{3,2,1,0:T(2,128)S(1)}, s32[2,4,2,128]{3,2,1,0:T(2,128)}, u32[]{:S(2)}) copy-start(s32[2,4,2,128]{3,2,1,0:T(2,128)} %half_ref.1) | copy-start | bytes 24580
  89.0 0.7 copy-start.5
  89.0 0.7 copy-start.6
where the time goes:
time: 102 us; the launch traced here: 103 us
  Pallas kernels  98.1 us (96%)
  local copies, waits for them, and re-layouts  4.36 us (4%)
    pallas_call x4, Pallas kernels, force_call(): pl.pallas_call(functools.partial(force_kernel, step_tag, phase), out_shap...  54.4 us
    pallas_call x3, Pallas kernels, exchange_call(): pl.pallas_call(functools.partial(exchange_kernel, mesh_sizes()), out_shap...  20.4 us
    pallas_call x1, Pallas kernels, project_call(): pl.pallas_call(functools.partial(gather_kernel, sizes), out_shape=whole,...  11.7 us
    pallas_call x1, Pallas kernels, first_call(): pl.pallas_call(functools.partial(first_kernel, mesh_sizes()), out_shape=(...  9.89 us
    unnamed x15, local copies, waits for them, and re-layouts  4.36 us

commit v1 on v0

--- a/solution.py
+++ b/solution.py
@@ -28,7 +28,7 @@
 
 
 VMEM_SPEC = pl.BlockSpec(memory_space=pltpu.VMEM)
-SMEM_SPEC = pl.BlockSpec(memory_space=pltpu.SMEM)
+HBM_SPEC = pl.BlockSpec(memory_space=pltpu.HBM)
 
 
 def pair_terms(own, chunk, step_tag):
@@ -67,10 +67,13 @@
             for k in range(3):
                 mine = rows_x[k, 1 + ix, 1 + iz, 1 : 1 + cy, :]
                 there = mine < 0.1 * FAR
+                if k == 0:
+                    held = jnp.sum(jnp.where(there, 1.0, 0.0), axis=1, keepdims=True)
                 least = jnp.min(jnp.where(there, mine, FAR), axis=1, keepdims=True)
                 most = jnp.max(jnp.where(there, mine, -FAR), axis=1, keepdims=True)
                 low.append(least - 1.001 - 1e-6 * jnp.abs(least))
                 high.append(most + 1.001 + 1e-6 * jnp.abs(most))
+            base_ref[row : row + cy, :] = jnp.broadcast_to(held, (cy, LANES)).astype(jnp.int32)
             for n, offset in enumerate(NEAR):
                 keep = None
                 for k in range(3):
@@ -101,7 +104,7 @@
     entry = entry & (LANES - 1)
     bases = []
     running = jnp.zeros((cells, LANES), jnp.int32)
-    table = jnp.zeros((cells, LANES), jnp.int32)
+    table = base_ref[...]
     spot_cells = lax.broadcasted_iota(jnp.int32, (cells, LANES), 1)
     for n in range(len(NEAR)):
         bases.append(running)
@@ -115,7 +118,7 @@
     index_ref[...] = entry
 
 
-def force_kernel(step_tag, phase, count_ref, padded_ref, state_ref, *refs):
+def force_kernel(step_tag, phase, padded_ref, state_ref, *refs):
     if phase == 0:
         tile_out, index_ref, base_ref, *scratch = refs
     elif phase == 1:
@@ -137,16 +140,15 @@
         for k in range(3):
             shift = jnp.where(row_id == k, cell_edge * offset[k], shift)
         shifts[n] = shift
-    eye = lax.broadcasted_iota(jnp.int32, (LANES, LANES), 0) == lax.broadcasted_iota(
-        jnp.int32, (LANES, LANES), 1
-    )
+    force_wide[...] = jnp.zeros(force_wide.shape, jnp.float32)
     zero = jnp.zeros((BLOCK, LANES), jnp.float32)
     to_smem.wait()
 
-    def one_cell(cell, carry):
-        ix = cell // (cy * cz)
-        iz = (cell // cy) % cz
-        iy = cell % cy
+    def place(cell):
+        return cell // (cy * cz), cell % cy, (cell // cy) % cz
+
+    def prepare(cell, slot):
+        ix, iy, iz = place(cell)
         current = jnp.zeros((ROWS, LANES), jnp.float32)
         for n, offset in enumerate(NEAR):
             tile = padded_ref[ix + 1 + offset[0], iy + 1 + offset[1], iz + 1 + offset[2]]
@@ -155,27 +157,32 @@
             base = base_smem[cell, n]
             following = base_smem[cell, n + 1]
             merged = jnp.where(lane >= (base & (LANES - 1)), found, current)
-            list_ref[base >> 7] = merged
+            list_ref[slot, base >> 7] = merged
             crossed = (following >> 7) > (base >> 7)
             current = jnp.where(crossed, found, merged)
         total = base_smem[cell, len(NEAR)]
-        list_ref[total >> 7] = jnp.where(
+        list_ref[slot, total >> 7] = jnp.where(
             (row_id == 0) & (lane >= (total & (LANES - 1))), -FAR, current
         )
-        chunks = (total + LANES - 1) >> 7
-        own_tile = padded_ref[ix + 1, iy + 1, iz + 1]
-        own_cols = own_tile.T
+        own_cols = padded_ref[ix + 1, iy + 1, iz + 1].T
         for k in range(7):
-            own_wide[k] = jnp.broadcast_to(own_cols[:, k : k + 1], (LANES, LANES))
-        blocks = (count_ref[ix, iy, iz] + BLOCK - 1) // BLOCK
+            own_wide[slot, k] = jnp.broadcast_to(own_cols[:, k : k + 1], (LANES, LANES))
+
+    prepare(0, 0)
+
+    def one_cell(cell, carry):
+        ix, iy, iz = place(cell)
+        slot = cell & 1
+        chunks = (base_smem[cell, len(NEAR)] + LANES - 1) >> 7
+        blocks = (base_smem[cell, len(NEAR) + 1] + BLOCK - 1) // BLOCK
 
         def one_block(block, carry):
             at = pl.multiple_of(block * BLOCK, BLOCK)
-            own = [own_wide[k, pl.ds(at, BLOCK), :] for k in range(7)]
+            own = [own_wide[slot, k, pl.ds(at, BLOCK), :] for k in range(7)]
             own[6] = own[6] * (1.0 / hash_prime)
 
             def one_chunk(index, sums):
-                chunk = [list_ref[index, k : k + 1, :] for k in range(7)]
+                chunk = [list_ref[slot, index, k : k + 1, :] for k in range(7)]
                 terms = pair_terms(own, chunk, step_tag)
                 return tuple(sums[k] + terms[k] for k in range(3))
 
@@ -185,11 +192,21 @@
             return carry
 
         lax.fori_loop(0, blocks, one_block, 0)
+        prepare(jnp.minimum(cell + 1, cells - 1), 1 - slot)
+        own_tile = padded_ref[ix + 1, iy + 1, iz + 1]
+        wide = force_wide[...].reshape(3 * LANES, LANES)
+        coarse = wide.astype(jnp.bfloat16)
+        fine = (wide - coarse.astype(jnp.float32)).astype(jnp.bfloat16)
+        summed = lax.dot_general(
+            jnp.ones((ROWS, 2 * LANES), jnp.bfloat16),
+            jnp.concatenate([coarse, fine], axis=1),
+            (((1,), (1,)), ((), ())),
+            preferred_element_type=jnp.float32,
+        )
         state = state_ref[ix, iy, iz]
         new_vel, force = [], []
         for k in range(3):
-            column = jnp.sum(force_wide[k], axis=1, keepdims=True)
-            row = jnp.sum(jnp.where(eye, column, 0.0), axis=0, keepdims=True)
+            row = summed[0:1, k * LANES : (k + 1) * LANES]
             row = jnp.where(own_tile[7:8, :] > 0.5, row, 0.0)
             force.append(row)
             new_vel.append(
@@ -224,7 +241,7 @@
     lax.fori_loop(0, cells, one_cell, 0)
 
 
-def force_call(step_tag, phase, cell_count, padded, state, *selection):
+def force_call(step_tag, phase, padded, state, *selection):
     px, py, pz = padded.shape[:3]
     cx, cy, cz = state.shape[:3]
     cells = cx * cy * cz
@@ -240,21 +257,21 @@
     return pl.pallas_call(
         functools.partial(force_kernel, step_tag, phase),
         out_shape=outs,
-        in_specs=[SMEM_SPEC] + [VMEM_SPEC] * (2 + len(selection)),
+        in_specs=[VMEM_SPEC] * (2 + len(selection)),
         out_specs=(VMEM_SPEC,) * len(outs),
         scratch_shapes=[
             pltpu.VMEM((3, px, pz, tall, LANES), jnp.float32),
             pltpu.VMEM((near * cells, LANES), jnp.float32),
             pltpu.VMEM((near, ROWS, LANES), jnp.float32),
             pltpu.SMEM((cells, LANES), jnp.int32),
-            pltpu.VMEM((near + 1, ROWS, LANES), jnp.float32),
-            pltpu.VMEM((7, LANES, LANES), jnp.float32),
+            pltpu.VMEM((2, near + 1, ROWS, LANES), jnp.float32),
+            pltpu.VMEM((2, 7, LANES, LANES), jnp.float32),
             pltpu.VMEM((3, LANES, LANES), jnp.float32),
             pltpu.SemaphoreType.DMA,
         ],
         compiler_params=pltpu.CompilerParams(vmem_limit_bytes=32 * 1024 * 1024),
         name="pair_forces",
-    )(cell_count, padded, state, *selection)
+    )(padded, state, *selection)
 
 
 MESH = pl.DeviceIdType.MESH
@@ -347,13 +364,27 @@
 
 
 def first_kernel(
-    sizes, count_ref, pos_ref, vel_ref, force_ref, seed_ref, padded_ref, state_ref,
-    tile_ref, send_sems, recv_sems,
+    sizes, count_hbm, pos_hbm, vel_hbm, force_hbm, seed_hbm, padded_ref, state_ref,
+    count_ref, pos_ref, vel_ref, force_ref, seed_ref, load_sems, tile_ref, send_sems, recv_sems,
 ):
+    loads = []
+    for number, (source, target) in enumerate(
+        (
+            (count_hbm, count_ref),
+            (pos_hbm, pos_ref),
+            (vel_hbm, vel_ref),
+            (force_hbm, force_ref),
+            (seed_hbm, seed_ref),
+        )
+    ):
+        loads.append(pltpu.make_async_copy(source, target, load_sems.at[number]))
+        loads[-1].start()
     cx, cy, cz = tile_ref.shape[:3]
     slot = lax.broadcasted_iota(jnp.int32, (1, LANES), 1)
 
     def fill():
+        for load in loads:
+            load.wait()
         for ix in range(cx):
             for iy in range(cy):
                 for iz in range(cz):
@@ -415,18 +446,33 @@
             jax.ShapeDtypeStruct(padded_shape(extent), jnp.float32),
             jax.ShapeDtypeStruct(extent + (ROWS, LANES), jnp.float32),
         ),
-        in_specs=[SMEM_SPEC] + [VMEM_SPEC] * 4,
+        in_specs=[HBM_SPEC] * 5,
         out_specs=(VMEM_SPEC, VMEM_SPEC),
-        scratch_shapes=[pltpu.VMEM(extent + (ROWS, LANES), jnp.float32)] + exchange_sems(),
+        scratch_shapes=[
+            pltpu.SMEM(extent, jnp.int32),
+            pltpu.VMEM(bead_pos.shape, jnp.float32),
+            pltpu.VMEM(bead_pos.shape, jnp.float32),
+            pltpu.VMEM(bead_pos.shape, jnp.float32),
+            pltpu.VMEM(pair_seed.shape, jnp.int32),
+            pltpu.SemaphoreType.DMA((5,)),
+            pltpu.VMEM(extent + (ROWS, LANES), jnp.float32),
+        ]
+        + exchange_sems(),
         compiler_params=comm_params(2),
         name="first_exchange",
     )(cell_count, bead_pos, bead_vel, bead_force, pair_seed)
 
 
 def gather_kernel(
-    sizes, state_ref, half_ref, grid_ref, map_ref, whole,
-    mine, along_z, along_y, slots_z, slots_y, send_sems, recv_sems,
+    sizes, state_ref, half_hbm, grid_hbm, map_hbm, whole,
+    half_ref, grid_ref, map_ref, load_sems, mine, plane, slots, send_sems, recv_sems,
 ):
+    loads = []
+    for number, (source, target) in enumerate(
+        ((half_hbm, half_ref), (grid_hbm, grid_ref), (map_hbm, map_ref))
+    ):
+        loads.append(pltpu.make_async_copy(source, target, load_sems.at[number]))
+        loads[-1].start()
     nx, ny, nz = sizes
     cx, cy, cz = state_ref.shape[:3]
     rows, depth = grid_ref.shape[2:]
@@ -434,15 +480,19 @@
     count_y = span // depth
     here = (lax.axis_index("gx"), lax.axis_index("gy"), lax.axis_index("gz"))
     barrier = pltpu.get_barrier_semaphore()
-    peers = []
-    for axis, size in ((2, nz), (1, ny), (0, nx)):
-        for step in range(1, size):
-            target = list(here)
-            target[axis] = lax.rem(here[axis] + step, size)
-            peers.append((axis, step, tuple(target)))
-    for axis, step, target in peers:
+    across, along = [], []
+    for step_y in range(ny):
+        for step_z in range(nz):
+            if step_y + step_z > 0:
+                place_y = lax.rem(here[1] + step_y, ny)
+                across.append((here[0], place_y, lax.rem(here[2] + step_z, nz)))
+    for step in range(1, nx):
+        along.append((lax.rem(here[0] + step, nx), here[1], here[2]))
+    for target in across + along:
         pl.semaphore_signal(barrier, inc=1, device_id=target, device_id_type=MESH)
 
+    for load in loads:
+        load.wait()
     lane = lax.broadcasted_iota(jnp.int32, (ROWS, span), 1)
     row_id = lax.broadcasted_iota(jnp.int32, (ROWS, LANES), 0)
     for ix in range(cx):
@@ -468,43 +518,39 @@
                     placed = placed + jnp.where(lane == at, total, 0.0)
         mine[ix] = placed
 
-    pl.semaphore_wait(barrier, len(peers))
-    number = 0
-    for axis, source, slots, size, result in (
-        (2, mine, slots_z, nz, along_z),
-        (1, along_z, slots_y, ny, along_y),
-        (0, along_y, None, nx, None),
-    ):
+    pl.semaphore_wait(barrier, len(across) + len(along))
+
+    def send_all(targets, source, landings, first):
         copies = []
-        for peer_axis, step, target in peers:
-            if peer_axis != axis:
-                continue
-            if axis == 0:
-                landing = whole.at[pl.ds(here[0] * cx, cx)]
-            else:
-                landing = slots.at[step - 1]
+        for number, target in enumerate(targets):
             copies.append(
                 pltpu.make_async_remote_copy(
                     src_ref=source,
-                    dst_ref=landing,
-                    send_sem=send_sems.at[number],
-                    recv_sem=recv_sems.at[number],
+                    dst_ref=landings[number],
+                    send_sem=send_sems.at[first + number],
+                    recv_sem=recv_sems.at[first + number],
                     device_id=target,
                     device_id_type=MESH,
                 )
             )
-            number += 1
         for copy in copies:
             copy.start()
-        if axis == 0:
-            whole[pl.ds(here[0] * cx, cx)] = source[...]
-        for copy in copies:
-            copy.wait()
-        if axis != 0:
-            total = source[...]
-            for step in range(1, size):
-                total = total + slots[step - 1]
-            result[...] = total
+        return copies
+
+    copies = send_all(across, mine, [slots.at[k] for k in range(len(across))], 0)
+    for copy in copies:
+        copy.wait_recv()
+    total = mine[...]
+    for number in range(len(across)):
+        total = total + slots[number]
+    plane[...] = total
+    band = pl.ds(here[0] * cx, cx)
+    later = send_all(along, plane, [whole.at[band]] * len(along), len(across))
+    whole[band] = total
+    for copy in later:
+        copy.wait()
+    for copy in copies:
+        copy.wait_send()
 
 
 def project_kernel(sizes, extent, rows, depth, whole, grid_out, pressure_out, brick_out, fields):
@@ -584,21 +630,24 @@
     depth = grid_vel.shape[3]
     span = ny * cy * depth
     shape = (cx, ROWS, span)
-    peers = nx + ny + nz - 3
+    across = max(ny * nz - 1, 1)
+    peers = max(ny * nz + nx - 2, 1)
     whole = jax.ShapeDtypeStruct((nx * cx, ROWS, span), jnp.float32)
     gathered = pl.pallas_call(
         functools.partial(gather_kernel, sizes),
         out_shape=whole,
-        in_specs=[VMEM_SPEC] * 4,
+        in_specs=[VMEM_SPEC] + [HBM_SPEC] * 3,
         out_specs=VMEM_SPEC,
         scratch_shapes=[
+            pltpu.VMEM(bead_half.shape, jnp.int32),
+            pltpu.VMEM(grid_vel.shape, jnp.float32),
+            pltpu.VMEM(correlation_map.shape, jnp.int32),
+            pltpu.SemaphoreType.DMA((3,)),
             pltpu.VMEM(shape, jnp.float32),
             pltpu.VMEM(shape, jnp.float32),
-            pltpu.VMEM(shape, jnp.float32),
-            pltpu.VMEM((max(nz - 1, 1),) + shape, jnp.float32),
-            pltpu.VMEM((max(ny - 1, 1),) + shape, jnp.float32),
-            pltpu.SemaphoreType.DMA((max(peers, 1),)),
-            pltpu.SemaphoreType.DMA((max(peers, 1),)),
+            pltpu.VMEM((across,) + shape, jnp.float32),
+            pltpu.SemaphoreType.DMA((peers,)),
+            pltpu.SemaphoreType.DMA((peers,)),
         ],
         compiler_params=comm_params(3),
         name="gather_grid",
@@ -626,11 +675,11 @@
         step_tag = step_number + 3
         if step_number > 0:
             padded = exchange_call(tile)
-        tile, *selection = force_call(step_tag, 0, cell_count, padded, state)
+        tile, *selection = force_call(step_tag, 0, padded, state)
         padded = exchange_call(tile)
         if step_number < STEPS - 1:
-            tile, state = force_call(step_tag, 1, cell_count, padded, state, *selection)
-    state, position, velocity = force_call(step_tag, 2, cell_count, padded, state, *selection)
+            tile, state = force_call(step_tag, 1, padded, state, *selection)
+    state, position, velocity = force_call(step_tag, 2, padded, state, *selection)
     return (position, velocity, *project_call(state, bead_half, grid_vel, correlation_map))
 
 

time: 102 us -> 93.2 us (0.914); the launches traced: 103 us -> 92.8 us
  Pallas kernels: 98.1 us -> 87.7 us
    pallas_call x4, Pallas kernels: 54.4 us -> 41.3 us  [force_call(): pl.pallas_call(functools.partial(force_kernel, step_tag, phase), out_shap...]
    pallas_call x3, Pallas kernels: 20.4 us -> 25 us  [exchange_call(): pl.pallas_call(functools.partial(exchange_kernel, mesh_sizes()), out_shap...]
    pallas_call x1, Pallas kernels: 11.7 us -> 10.2 us  [project_call(): pl.pallas_call(functools.partial(gather_kernel, sizes), out_shape=whole,...]
where the time goes in v1:
time: 93.2 us; the launch traced here: 92.8 us
  Pallas kernels  87.7 us (94%)
  local copies, waits for them, and re-layouts  4.36 us (5%)
    pallas_call x4, Pallas kernels, force_call(): pl.pallas_call(functools.partial(force_kernel, step_tag, phase), out_shap...  41.3 us
    pallas_call x3, Pallas kernels, exchange_call(): pl.pallas_call(functools.partial(exchange_kernel, mesh_sizes()), out_shap...  25 us
    pallas_call x1, Pallas kernels, project_call(): pl.pallas_call(functools.partial(gather_kernel, sizes), out_shape=whole,...  10.2 us
    pallas_call x1, Pallas kernels, first_call(): pl.pallas_call(functools.partial(first_kernel, mesh_sizes()), out_shape=(...  9.41 us
    unnamed x15, local copies, waits for them, and re-layouts  4.36 us

profile of v1, /device:TPU:0, one launch (start us, length us, event | category | flops | bytes accessed | tf_op | source)
XLA Modules:
  0.0 92.8 jit_solution(16451826392671748861)
XLA Ops:
  0.6 0.8 copy.13.count_hbm
  1.4 0.0 copy-start
  1.4 0.7 copy-done
  2.1 0.0 copy-start.1
  2.1 0.7 copy-done.1
  2.9 0.0 copy-start.2
  2.9 0.7 copy-done.2
  3.6 0.0 copy-start.4
  3.6 0.7 copy-done.4
  4.3 9.4 %first_exchange.1 = (f32[4,6,4,8,128]{4,3,2,1,0:T(8,128)S(1)}, f32[2,4,2,8,128]{4,3,2,1,0:T(8,128)S(1)}) custom-call(s32[2,4,2]{2,1,0:T(4,128)S(1)} %copy.13.count_hbm, f32[3,2,4,2,128]{4,3,2,1,0:T(2,128)S(1)} %copy-done, f32[3,2,4,2,128]{4,3,2,1,0:T(2,128)S(1)} %copy-done.1, f32[3,2,4,2,128]{4,3,2,1,0:T(2,128)S(1)} %copy-done.2, s32[2,4,2,128]{3,2,1,0:T(2,128)S(1)} %copy-done.4), custom_call_target="tpu_custom_call" | custom-call | tf_op jit(solution)/shard_map/first_exchange/pallas_call | solution.py:443
  13.7 10.9 %pair_forces.4 = (f32[2,4,2,8,128]{4,3,2,1,0:T(8,128)S(1)}, s32[432,128]{1,0:T(8,128)S(1)}, s32[16,128]{1,0:T(8,128)S(1)}) custom-call(f32[4,6,4,8,128]{4,3,2,1,0:T(8,128)S(1)} %get-tuple-element.21.padded_ref, f32[2,4,2,8,128]{4,3,2,1,0:T(8,128)S(1)} %get-tuple-element.22.state_ref), custom_call_target="tpu_custom_call" | custom-call | tf_op jit(solution)/shard_map/pair_forces/pallas_call | solution.py:257
  24.7 8.2 %exchange.3.padded_ref = f32[4,6,4,8,128]{4,3,2,1,0:T(8,128)S(1)} custom-call(f32[2,4,2,8,128]{4,3,2,1,0:T(8,128)S(1)} %get-tuple-element.23.tile_ref), custom_call_target="tpu_custom_call" | custom-call | tf_op jit(solution)/shard_map/exchange/pallas_call | solution.py:430
  32.9 9.5 %pair_forces.5 = (f32[2,4,2,8,128]{4,3,2,1,0:T(8,128)S(1)}, f32[2,4,2,8,128]{4,3,2,1,0:T(8,128)S(1)}) custom-call(f32[4,6,4,8,128]{4,3,2,1,0:T(8,128)S(1)} %exchange.3.padded_ref, f32[2,4,2,8,128]{4,3,2,1,0:T(8,128)S(1)} %get-tuple-element.22.state_ref, s32[432,128]{1,0:T(8,128)S(1)} %get-tuple-element.24.refs_0_, s32[16,128]{1,0:T(8,128)S(1)} %get-tuple-element.25.refs_1_), custom_call_target="tpu_custom_call" | custom-call | tf_op jit(solution)/shard_map/pair_forces/pallas_call | solution.py:257
  42.3 8.4 %exchange.4.padded_ref = f32[4,6,4,8,128]{4,3,2,1,0:T(8,128)S(1)} custom-call(f32[2,4,2,8,128]{4,3,2,1,0:T(8,128)S(1)} %get-tuple-element.26.tile_ref), custom_call_target="tpu_custom_call" | custom-call | tf_op jit(solution)/shard_map/exchange/pallas_call | solution.py:430
  50.7 10.9 %pair_forces.6 = (f32[2,4,2,8,128]{4,3,2,1,0:T(8,128)S(1)}, s32[432,128]{1,0:T(8,128)S(1)}, s32[16,128]{1,0:T(8,128)S(1)}) custom-call(f32[4,6,4,8,128]{4,3,2,1,0:T(8,128)S(1)} %exchange.4.padded_ref, f32[2,4,2,8,128]{4,3,2,1,0:T(8,128)S(1)} %get-tuple-element.27.state_ref), custom_call_target="tpu_custom_call" | custom-call | tf_op jit(solution)/shard_map/pair_forces/pallas_call | solution.py:257
  61.6 8.5 %exchange.5.padded_ref = f32[4,6,4,8,128]{4,3,2,1,0:T(8,128)S(1)} custom-call(f32[2,4,2,8,128]{4,3,2,1,0:T(8,128)S(1)} %get-tuple-element.28.tile_ref), custom_call_target="tpu_custom_call" | custom-call | tf_op jit(solution)/shard_map/exchange/pallas_call | solution.py:430
  70.1 0.0 copy-start.3
  70.2 10.0 %pair_forces.7 = (f32[2,4,2,8,128]{4,3,2,1,0:T(8,128)S(1)}, f32[3,2,4,2,128]{4,3,2,1,0:T(2,128)}, f32[3,2,4,2,128]{4,3,2,1,0:T(2,128)}) custom-call(f32[4,6,4,8,128]{4,3,2,1,0:T(8,128)S(1)} %exchange.5.padded_ref, f32[2,4,2,8,128]{4,3,2,1,0:T(8,128)S(1)} %get-tuple-element.27.state_ref, s32[432,128]{1,0:T(8,128)S(1)} %get-tuple-element.29.refs_0_, ...), custom_call_target="tpu_custom_call" | custom-call | tf_op jit(solution)/shard_map/pair_forces/pallas_call | solution.py:257
  80.1 0.0 copy-start.5
  80.1 0.0 copy-start.6
  80.1 0.0 copy-done.3
  80.2 0.7 copy-done.5
  80.8 0.0 copy-done.6
  80.8 10.2 %gather_grid.1.whole = f32[8,8,128]{2,1,0:T(8,128)S(1)} custom-call(f32[2,4,2,8,128]{4,3,2,1,0:T(8,128)S(1)} %get-tuple-element.33.state_ref, s32[2,4,2,128]{3,2,1,0:T(2,128)S(1)} %copy-done.3, f32[3,2,1,16]{3,2,1,0:T(1,128)S(1)} %copy-done.5, s32[2,1,16]{2,1,0:T(1,128)S(1)} %copy-done.6), custom_call_target="tpu_custom_call" | custom-call | tf_op jit(solution)/shard_map/gather_grid/pallas_call | solution.py:636
  91.0 1.8 %project.1 = (f32[3,2,1,16]{3,2,1,0:T(1,128)}, f32[2,1,16]{2,1,0:T(1,128)}, f32[3,2,4,4]{3,2,1,0:T(4,128)}) custom-call(f32[8,8,128]{2,1,0:T(8,128)S(1)} %gather_grid.1.whole), custom_call_target="tpu_custom_call" | custom-call | tf_op jit(solution)/shard_map/project/pallas_call | solution.py:655
Async XLA Ops:
  1.4 0.7 copy-start
  2.1 0.7 copy-start.1
  2.9 0.7 copy-start.2
  3.6 0.7 copy-start.4
  70.1 10.0 %copy-start.3 = (s32[2,4,2,128]{3,2,1,0:T(2,128)S(1)}, s32[2,4,2,128]{3,2,1,0:T(2,128)}, u32[]{:S(2)}) copy-start(s32[2,4,2,128]{3,2,1,0:T(2,128)} %half_hbm.1) | copy-start | bytes 24580
  80.1 0.7 copy-start.5
  80.1 0.7 copy-start.6

commit v2 on v1

--- a/solution.py
+++ b/solution.py
@@ -125,7 +125,7 @@
         index_ref, base_ref, tile_out, state_out, *scratch = refs
     else:
         index_ref, base_ref, state_out, pos_out, vel_out, *scratch = refs
-    rows_x, masks, shifts, base_smem, list_ref, own_wide, force_wide, copy_sem = scratch
+    rows_x, masks, shifts, base_smem, list_ref, own_wide, force_wide, spreader, copy_sem = scratch
     px, py, pz = padded_ref.shape[:3]
     cx, cy, cz = px - 2, py - 2, pz - 2
     cells = cx * cy * cz
@@ -141,6 +141,9 @@
             shift = jnp.where(row_id == k, cell_edge * offset[k], shift)
         shifts[n] = shift
     force_wide[...] = jnp.zeros(force_wide.shape, jnp.float32)
+    from_row = lax.broadcasted_iota(jnp.int32, spreader.shape, 0) & (ROWS - 1)
+    to_part = lax.broadcasted_iota(jnp.int32, spreader.shape, 1) >> 7
+    spreader[...] = jnp.where(from_row == to_part, 1.0, 0.0).astype(jnp.bfloat16)
     zero = jnp.zeros((BLOCK, LANES), jnp.float32)
     to_smem.wait()
 
@@ -164,9 +167,16 @@
         list_ref[slot, total >> 7] = jnp.where(
             (row_id == 0) & (lane >= (total & (LANES - 1))), -FAR, current
         )
-        own_cols = padded_ref[ix + 1, iy + 1, iz + 1].T
+        own_tile = padded_ref[ix + 1, iy + 1, iz + 1]
+        parts, left = [], own_tile
+        for level in range(3):
+            parts.append(left.astype(jnp.bfloat16).astype(jnp.float32))
+            left = left - parts[-1]
+        parts.append(jnp.zeros_like(own_tile))
+        own_cols = jnp.concatenate(parts, axis=0).T.astype(jnp.bfloat16)
+        spread = jnp.dot(own_cols, spreader[...], preferred_element_type=jnp.float32)
         for k in range(7):
-            own_wide[slot, k] = jnp.broadcast_to(own_cols[:, k : k + 1], (LANES, LANES))
+            own_wide[slot, k] = spread[:, k * LANES : (k + 1) * LANES]
 
     prepare(0, 0)
 
@@ -267,6 +277,7 @@
             pltpu.VMEM((2, near + 1, ROWS, LANES), jnp.float32),
             pltpu.VMEM((2, 7, LANES, LANES), jnp.float32),
             pltpu.VMEM((3, LANES, LANES), jnp.float32),
+            pltpu.VMEM((4 * ROWS, 7 * LANES), jnp.bfloat16),
             pltpu.SemaphoreType.DMA,
         ],
         compiler_params=pltpu.CompilerParams(vmem_limit_bytes=32 * 1024 * 1024),
@@ -275,7 +286,10 @@
 
 
 MESH = pl.DeviceIdType.MESH
-AROUND = [offset for offset in NEAR if offset != (0, 0, 0)]
+AROUND = sorted(
+    (offset for offset in NEAR if offset != (0, 0, 0)),
+    key=lambda offset: sum(abs(step) for step in offset),
+)
 
 
 def when(condition, body):
@@ -392,7 +406,7 @@
                         ref[:, ix, iy, iz, :] for ref in (pos_ref, vel_ref, force_ref)
                     ]
                     seed = seed_ref[ix, iy, iz : iz + 1, :].astype(jnp.float32)
-                    here = jnp.where(slot < count_ref[ix, iy, iz], 1.0, 0.0)
+                    here = jnp.where(slot < count_ref[ix, iz, iy], 1.0, 0.0)
                     pos = pos + time_step * vel + 0.5 * time_step * time_step * force
                     guessed = vel + predict_weight * time_step * force
                     for ref, top, low, mark in (
@@ -449,7 +463,7 @@
         in_specs=[HBM_SPEC] * 5,
         out_specs=(VMEM_SPEC, VMEM_SPEC),
         scratch_shapes=[
-            pltpu.SMEM(extent, jnp.int32),
+            pltpu.SMEM((extent[0], extent[2], extent[1]), jnp.int32),
             pltpu.VMEM(bead_pos.shape, jnp.float32),
             pltpu.VMEM(bead_pos.shape, jnp.float32),
             pltpu.VMEM(bead_pos.shape, jnp.float32),
@@ -460,7 +474,7 @@
         + exchange_sems(),
         compiler_params=comm_params(2),
         name="first_exchange",
-    )(cell_count, bead_pos, bead_vel, bead_force, pair_seed)
+    )(jnp.swapaxes(cell_count, 1, 2), bead_pos, bead_vel, bead_force, pair_seed)
 
 
 def gather_kernel(

time: 93.2 us -> 95.6 us (1.026)
  Pallas kernels: 87.7 us -> 89.8 us
    pallas_call x4, Pallas kernels: 41.3 us -> 43 us  [force_call(): pl.pallas_call(functools.partial(force_kernel, step_tag, phase), out_shap...]
    unnamed x15 -> x16, local copies, waits for them, and re-layouts: 4.36 us -> 4.26 us
where the time goes in v2:
time: 95.6 us; the launch traced here: 94.8 us
  Pallas kernels  89.8 us (94%)
  local copies, waits for them, and re-layouts  4.26 us (4%)
    pallas_call x4, Pallas kernels, force_call(): pl.pallas_call(functools.partial(force_kernel, step_tag, phase), out_shap...  43 us
    pallas_call x3, Pallas kernels, exchange_call(): pl.pallas_call(functools.partial(exchange_kernel, mesh_sizes()), out_shap...  24.2 us
    pallas_call x1, Pallas kernels, project_call(): pl.pallas_call(functools.partial(gather_kernel, sizes), out_shape=whole,...  11 us
    pallas_call x1, Pallas kernels, first_call(): pl.pallas_call(functools.partial(first_kernel, mesh_sizes()), out_shape=(...  9.77 us
    unnamed x16, local copies, waits for them, and re-layouts  4.26 us

profile of v2, /device:TPU:0, one launch (start us, length us, event | category | flops | bytes accessed | tf_op | source)
XLA Modules:
  0.0 94.8 jit_solution(13706611596484763900)
XLA Ops:
  0.6 0.0 copy-start
  0.6 0.7 copy-done
  1.4 0.0 copy-start.1
  1.4 0.7 copy-done.1
  2.1 0.0 copy-start.2
  2.1 0.7 copy-done.2
  2.8 0.0 copy-start.4
  2.8 0.7 copy-done.4
  3.5 0.0 copy-start.6
  3.5 0.7 copy-done.6
  4.2 9.8 %first_exchange.1 = (f32[4,6,4,8,128]{4,3,2,1,0:T(8,128)S(1)}, f32[2,4,2,8,128]{4,3,2,1,0:T(8,128)S(1)}) custom-call(s32[2,2,4]{2,1,0:T(2,128)S(1)} %bitcast.1, f32[3,2,4,2,128]{4,3,2,1,0:T(2,128)S(1)} %copy-done, f32[3,2,4,2,128]{4,3,2,1,0:T(2,128)S(1)} %copy-done.1, f32[3,2,4,2,128]{4,3,2,1,0:T(2,128)S(1)} %copy-done.2, s32[2,4,2,128]{3,2,1,0:T(2,128)S(1)} %copy-done.4), custom_call_target="tpu_custom_call" | custom-call | tf_op jit(solution)/shard_map/first_exchange/pallas_call | solution.py:457
  14.0 11.4 %pair_forces.4 = (f32[2,4,2,8,128]{4,3,2,1,0:T(8,128)S(1)}, s32[432,128]{1,0:T(8,128)S(1)}, s32[16,128]{1,0:T(8,128)S(1)}) custom-call(f32[4,6,4,8,128]{4,3,2,1,0:T(8,128)S(1)} %get-tuple-element.21.padded_ref, f32[2,4,2,8,128]{4,3,2,1,0:T(8,128)S(1)} %get-tuple-element.22.state_ref), custom_call_target="tpu_custom_call" | custom-call | tf_op jit(solution)/shard_map/pair_forces/pallas_call | solution.py:267
  25.4 8.0 %exchange.3.padded_ref = f32[4,6,4,8,128]{4,3,2,1,0:T(8,128)S(1)} custom-call(f32[2,4,2,8,128]{4,3,2,1,0:T(8,128)S(1)} %get-tuple-element.23.tile_ref), custom_call_target="tpu_custom_call" | custom-call | tf_op jit(solution)/shard_map/exchange/pallas_call | solution.py:444
  33.3 9.9 %pair_forces.5 = (f32[2,4,2,8,128]{4,3,2,1,0:T(8,128)S(1)}, f32[2,4,2,8,128]{4,3,2,1,0:T(8,128)S(1)}) custom-call(f32[4,6,4,8,128]{4,3,2,1,0:T(8,128)S(1)} %exchange.3.padded_ref, f32[2,4,2,8,128]{4,3,2,1,0:T(8,128)S(1)} %get-tuple-element.22.state_ref, s32[432,128]{1,0:T(8,128)S(1)} %get-tuple-element.24.refs_0_, s32[16,128]{1,0:T(8,128)S(1)} %get-tuple-element.25.refs_1_), custom_call_target="tpu_custom_call" | custom-call | tf_op jit(solution)/shard_map/pair_forces/pallas_call | solution.py:267
  43.3 8.1 %exchange.4.padded_ref = f32[4,6,4,8,128]{4,3,2,1,0:T(8,128)S(1)} custom-call(f32[2,4,2,8,128]{4,3,2,1,0:T(8,128)S(1)} %get-tuple-element.26.tile_ref), custom_call_target="tpu_custom_call" | custom-call | tf_op jit(solution)/shard_map/exchange/pallas_call | solution.py:444
  51.4 11.3 %pair_forces.6 = (f32[2,4,2,8,128]{4,3,2,1,0:T(8,128)S(1)}, s32[432,128]{1,0:T(8,128)S(1)}, s32[16,128]{1,0:T(8,128)S(1)}) custom-call(f32[4,6,4,8,128]{4,3,2,1,0:T(8,128)S(1)} %exchange.4.padded_ref, f32[2,4,2,8,128]{4,3,2,1,0:T(8,128)S(1)} %get-tuple-element.27.state_ref), custom_call_target="tpu_custom_call" | custom-call | tf_op jit(solution)/shard_map/pair_forces/pallas_call | solution.py:267
  62.7 8.1 %exchange.5.padded_ref = f32[4,6,4,8,128]{4,3,2,1,0:T(8,128)S(1)} custom-call(f32[2,4,2,8,128]{4,3,2,1,0:T(8,128)S(1)} %get-tuple-element.28.tile_ref), custom_call_target="tpu_custom_call" | custom-call | tf_op jit(solution)/shard_map/exchange/pallas_call | solution.py:444
  70.8 0.0 copy-start.3
  70.8 10.4 %pair_forces.7 = (f32[2,4,2,8,128]{4,3,2,1,0:T(8,128)S(1)}, f32[3,2,4,2,128]{4,3,2,1,0:T(2,128)}, f32[3,2,4,2,128]{4,3,2,1,0:T(2,128)}) custom-call(f32[4,6,4,8,128]{4,3,2,1,0:T(8,128)S(1)} %exchange.5.padded_ref, f32[2,4,2,8,128]{4,3,2,1,0:T(8,128)S(1)} %get-tuple-element.27.state_ref, s32[432,128]{1,0:T(8,128)S(1)} %get-tuple-element.29.refs_0_, ...), custom_call_target="tpu_custom_call" | custom-call | tf_op jit(solution)/shard_map/pair_forces/pallas_call | solution.py:267
  81.3 0.0 copy-start.5
  81.3 0.0 copy-start.7
  81.3 0.0 copy-done.3
  81.3 0.7 copy-done.5
  82.0 0.0 copy-done.7
  82.0 11.0 %gather_grid.1.whole = f32[8,8,128]{2,1,0:T(8,128)S(1)} custom-call(f32[2,4,2,8,128]{4,3,2,1,0:T(8,128)S(1)} %get-tuple-element.33.state_ref, s32[2,4,2,128]{3,2,1,0:T(2,128)S(1)} %copy-done.3, f32[3,2,1,16]{3,2,1,0:T(1,128)S(1)} %copy-done.5, s32[2,1,16]{2,1,0:T(1,128)S(1)} %copy-done.7), custom_call_target="tpu_custom_call" | custom-call | tf_op jit(solution)/shard_map/gather_grid/pallas_call | solution.py:650
  93.0 1.8 %project.1 = (f32[3,2,1,16]{3,2,1,0:T(1,128)}, f32[2,1,16]{2,1,0:T(1,128)}, f32[3,2,4,4]{3,2,1,0:T(4,128)}) custom-call(f32[8,8,128]{2,1,0:T(8,128)S(1)} %gather_grid.1.whole), custom_call_target="tpu_custom_call" | custom-call | tf_op jit(solution)/shard_map/project/pallas_call | solution.py:669
Async XLA Ops:
  0.6 0.7 copy-start
  1.4 0.7 copy-start.1
  2.1 0.7 copy-start.2
  2.8 0.7 copy-start.4
  3.5 0.7 copy-start.6
  70.8 10.5 %copy-start.3 = (s32[2,4,2,128]{3,2,1,0:T(2,128)S(1)}, s32[2,4,2,128]{3,2,1,0:T(2,128)}, u32[]{:S(2)}) copy-start(s32[2,4,2,128]{3,2,1,0:T(2,128)} %half_hbm.1) | copy-start | bytes 24580
  81.3 0.7 copy-start.5
  81.3 0.7 copy-start.7

commit v3 on v1

--- a/solution.py
+++ b/solution.py
@@ -170,7 +170,7 @@
 
     prepare(0, 0)
 
-    def one_cell(cell, carry):
+    def one_cell(cell, carry, more=True):
         ix, iy, iz = place(cell)
         slot = cell & 1
         chunks = (base_smem[cell, len(NEAR)] + LANES - 1) >> 7
@@ -192,7 +192,8 @@
             return carry
 
         lax.fori_loop(0, blocks, one_block, 0)
-        prepare(jnp.minimum(cell + 1, cells - 1), 1 - slot)
+        if more:
+            prepare(cell + 1, 1 - slot)
         own_tile = padded_ref[ix + 1, iy + 1, iz + 1]
         wide = force_wide[...].reshape(3 * LANES, LANES)
         coarse = wide.astype(jnp.bfloat16)
@@ -238,7 +239,8 @@
             tile_out[ix, iy, iz, 7:8, :] = state[7:8, :]
         return carry
 
-    lax.fori_loop(0, cells, one_cell, 0)
+    lax.fori_loop(0, cells - 1, one_cell, 0)
+    one_cell(jnp.int32(cells - 1), 0, more=False)
 
 
 def force_call(step_tag, phase, padded, state, *selection):

time: 93.2 us -> 91.7 us (0.984)
  no operation moved by 1% of the time
where the time goes in v3:
time: 91.7 us; the launch traced here: 91.9 us
  Pallas kernels  86.8 us (95%)
  local copies, waits for them, and re-layouts  4.36 us (5%)
    pallas_call x4, Pallas kernels, force_call(): pl.pallas_call(functools.partial(force_kernel, step_tag, phase), out_shap...  40.7 us
    pallas_call x3, Pallas kernels, exchange_call(): pl.pallas_call(functools.partial(exchange_kernel, mesh_sizes()), out_shap...  25 us
    pallas_call x1, Pallas kernels, project_call(): pl.pallas_call(functools.partial(gather_kernel, sizes), out_shape=whole,...  9.85 us
    pallas_call x1, Pallas kernels, first_call(): pl.pallas_call(functools.partial(first_kernel, mesh_sizes()), out_shape=(...  9.41 us
    unnamed x15, local copies, waits for them, and re-layouts  4.36 us

profile of v3, /device:TPU:0, one launch (start us, length us, event | category | flops | bytes accessed | tf_op | source)
XLA Modules:
  0.0 91.9 jit_solution(7992369957193791048)
XLA Ops:
  0.6 0.8 copy.13.count_hbm
  1.4 0.0 copy-start
  1.4 0.7 copy-done
  2.1 0.0 copy-start.1
  2.1 0.7 copy-done.1
  2.9 0.0 copy-start.2
  2.9 0.7 copy-done.2
  3.6 0.0 copy-start.4
  3.6 0.7 copy-done.4
  4.3 9.4 %first_exchange.1 = (f32[4,6,4,8,128]{4,3,2,1,0:T(8,128)S(1)}, f32[2,4,2,8,128]{4,3,2,1,0:T(8,128)S(1)}) custom-call(s32[2,4,2]{2,1,0:T(4,128)S(1)} %copy.13.count_hbm, f32[3,2,4,2,128]{4,3,2,1,0:T(2,128)S(1)} %copy-done, f32[3,2,4,2,128]{4,3,2,1,0:T(2,128)S(1)} %copy-done.1, f32[3,2,4,2,128]{4,3,2,1,0:T(2,128)S(1)} %copy-done.2, s32[2,4,2,128]{3,2,1,0:T(2,128)S(1)} %copy-done.4), custom_call_target="tpu_custom_call" | custom-call | tf_op jit(solution)/shard_map/first_exchange/pallas_call | solution.py:445
  13.7 10.7 %pair_forces.4 = (f32[2,4,2,8,128]{4,3,2,1,0:T(8,128)S(1)}, s32[432,128]{1,0:T(8,128)S(1)}, s32[16,128]{1,0:T(8,128)S(1)}) custom-call(f32[4,6,4,8,128]{4,3,2,1,0:T(8,128)S(1)} %get-tuple-element.21.padded_ref, f32[2,4,2,8,128]{4,3,2,1,0:T(8,128)S(1)} %get-tuple-element.22.state_ref), custom_call_target="tpu_custom_call" | custom-call | tf_op jit(solution)/shard_map/pair_forces/pallas_call | solution.py:259
  24.5 8.5 %exchange.3.padded_ref = f32[4,6,4,8,128]{4,3,2,1,0:T(8,128)S(1)} custom-call(f32[2,4,2,8,128]{4,3,2,1,0:T(8,128)S(1)} %get-tuple-element.23.tile_ref), custom_call_target="tpu_custom_call" | custom-call | tf_op jit(solution)/shard_map/exchange/pallas_call | solution.py:432
  33.0 9.3 %pair_forces.5 = (f32[2,4,2,8,128]{4,3,2,1,0:T(8,128)S(1)}, f32[2,4,2,8,128]{4,3,2,1,0:T(8,128)S(1)}) custom-call(f32[4,6,4,8,128]{4,3,2,1,0:T(8,128)S(1)} %exchange.3.padded_ref, f32[2,4,2,8,128]{4,3,2,1,0:T(8,128)S(1)} %get-tuple-element.22.state_ref, s32[432,128]{1,0:T(8,128)S(1)} %get-tuple-element.24.refs_0_, s32[16,128]{1,0:T(8,128)S(1)} %get-tuple-element.25.refs_1_), custom_call_target="tpu_custom_call" | custom-call | tf_op jit(solution)/shard_map/pair_forces/pallas_call | solution.py:259
  42.3 7.8 %exchange.4.padded_ref = f32[4,6,4,8,128]{4,3,2,1,0:T(8,128)S(1)} custom-call(f32[2,4,2,8,128]{4,3,2,1,0:T(8,128)S(1)} %get-tuple-element.26.tile_ref), custom_call_target="tpu_custom_call" | custom-call | tf_op jit(solution)/shard_map/exchange/pallas_call | solution.py:432
  50.1 10.9 %pair_forces.6 = (f32[2,4,2,8,128]{4,3,2,1,0:T(8,128)S(1)}, s32[432,128]{1,0:T(8,128)S(1)}, s32[16,128]{1,0:T(8,128)S(1)}) custom-call(f32[4,6,4,8,128]{4,3,2,1,0:T(8,128)S(1)} %exchange.4.padded_ref, f32[2,4,2,8,128]{4,3,2,1,0:T(8,128)S(1)} %get-tuple-element.27.state_ref), custom_call_target="tpu_custom_call" | custom-call | tf_op jit(solution)/shard_map/pair_forces/pallas_call | solution.py:259
  61.0 8.7 %exchange.5.padded_ref = f32[4,6,4,8,128]{4,3,2,1,0:T(8,128)S(1)} custom-call(f32[2,4,2,8,128]{4,3,2,1,0:T(8,128)S(1)} %get-tuple-element.28.tile_ref), custom_call_target="tpu_custom_call" | custom-call | tf_op jit(solution)/shard_map/exchange/pallas_call | solution.py:432
  69.6 0.0 copy-start.3
  69.7 9.9 %pair_forces.7 = (f32[2,4,2,8,128]{4,3,2,1,0:T(8,128)S(1)}, f32[3,2,4,2,128]{4,3,2,1,0:T(2,128)}, f32[3,2,4,2,128]{4,3,2,1,0:T(2,128)}) custom-call(f32[4,6,4,8,128]{4,3,2,1,0:T(8,128)S(1)} %exchange.5.padded_ref, f32[2,4,2,8,128]{4,3,2,1,0:T(8,128)S(1)} %get-tuple-element.27.state_ref, s32[432,128]{1,0:T(8,128)S(1)} %get-tuple-element.29.refs_0_, ...), custom_call_target="tpu_custom_call" | custom-call | tf_op jit(solution)/shard_map/pair_forces/pallas_call | solution.py:259
  79.5 0.0 copy-start.5
  79.6 0.0 copy-start.6
  79.6 0.0 copy-done.3
  79.6 0.7 copy-done.5
  80.2 0.0 copy-done.6
  80.2 9.8 %gather_grid.1.whole = f32[8,8,128]{2,1,0:T(8,128)S(1)} custom-call(f32[2,4,2,8,128]{4,3,2,1,0:T(8,128)S(1)} %get-tuple-element.33.state_ref, s32[2,4,2,128]{3,2,1,0:T(2,128)S(1)} %copy-done.3, f32[3,2,1,16]{3,2,1,0:T(1,128)S(1)} %copy-done.5, s32[2,1,16]{2,1,0:T(1,128)S(1)} %copy-done.6), custom_call_target="tpu_custom_call" | custom-call | tf_op jit(solution)/shard_map/gather_grid/pallas_call | solution.py:638
  90.1 1.8 %project.1 = (f32[3,2,1,16]{3,2,1,0:T(1,128)}, f32[2,1,16]{2,1,0:T(1,128)}, f32[3,2,4,4]{3,2,1,0:T(4,128)}) custom-call(f32[8,8,128]{2,1,0:T(8,128)S(1)} %gather_grid.1.whole), custom_call_target="tpu_custom_call" | custom-call | tf_op jit(solution)/shard_map/project/pallas_call | solution.py:657
Async XLA Ops:
  1.4 0.7 copy-start
  2.1 0.7 copy-start.1
  2.9 0.7 copy-start.2
  3.6 0.7 copy-start.4
  69.6 9.9 %copy-start.3 = (s32[2,4,2,128]{3,2,1,0:T(2,128)S(1)}, s32[2,4,2,128]{3,2,1,0:T(2,128)}, u32[]{:S(2)}) copy-start(s32[2,4,2,128]{3,2,1,0:T(2,128)} %half_hbm.1) | copy-start | bytes 24580
  79.5 0.7 copy-start.5
  79.6 0.7 copy-start.6
